TPU v7x, 128 devices: a whole 4x4x4 slice. The times are simulated.
128 devices in a mesh: grp: 16 (over x_hi, y, core), mem: 8 (over x_lo, z).
Axes of the slice: x: 4 (x_hi: 2, x_lo: 2; x = x_hi * 2 + x_lo), y: 4, z: 4, core: 2. Of those that a mesh axis runs over, the one named last changes fastest.
Arguments:
- q_branch: bfloat16 [16384, 4096], P(('grp', 'mem')), parts along dimension 0, may hold values from -6 to 6
- k_branch: bfloat16 [16384, 512], P(('grp', 'mem')), parts along dimension 0, may hold values from -6 to 6
- v_branch: bfloat16 [16384, 512], P(('grp', 'mem')), parts along dimension 0, may hold values from -6 to 6
- k_root: bfloat16 [32768, 512], P(('grp', 'mem')), parts along dimension 0, may hold values from -6 to 6
- v_root: bfloat16 [32768, 512], P(('grp', 'mem')), parts along dimension 0, may hold values from -6 to 6
- d_out: bfloat16 [16384, 4096], P(('grp', 'mem')), parts along dimension 0, may hold values from -6 to 6
- lengths: int32 [128, 4], P(('grp', 'mem')), parts along dimension 0, may hold values from 1 to 64, 128 in all within a row
- forks: int32 [128, 4], P(('grp', 'mem')), parts along dimension 0, may hold values from 2 to 2048
Outputs:
- dq_branch: bfloat16 [16384, 4096], P(('grp', 'mem')), parts along dimension 0
- dk_branch: bfloat16 [16384, 512], P(('grp', 'mem')), parts along dimension 0
- dv_branch: bfloat16 [16384, 512], P(('grp', 'mem')), parts along dimension 0
- dk_root: bfloat16 [32768, 512], P(('grp', 'mem')), parts along dimension 0
- dv_root: bfloat16 [32768, 512], P(('grp', 'mem')), parts along dimension 0
There are 16 independent parts, one for each index of `grp`. A program takes and returns all parts, laid end to end along the dimension named above; each array names one. Nothing has to cross between parts.
Inputs may be any that keep to these rules, and one draw needn't show every extreme that they name: Each row's 4 lengths sum to 128.
All inputs are finite; a program needn't handle non-finite values.
Results may differ from a plain program's by a relative error of at most 0.02.
Values may be sent and summed in bfloat16 or wider, within the bound.
A program may use at most 128 MiB of HBM per device.

v0:
```python
import functools
import math

import jax
import jax.numpy as jnp
from jax import lax
from jax.experimental import pallas as pl
from jax.experimental.pallas import tpu as pltpu
from jax.sharding import PartitionSpec as P

KVH = 4
GROUP = 8
HD = 128
TOK = 128
NQ = GROUP * TOK
SHARD = 256
HALF = SHARD // 2
N_MEM = 8
RING = 4
ROOT = SHARD * N_MEM
LT = 256
NEG = -1e30
SCALE = 1.0 / math.sqrt(HD)
C2 = SCALE / math.log(2.0)
SLOTS = 31
F32 = jnp.float32
BF16 = jnp.bfloat16
NT = (((1,), (1,)), ((), ()))


def kernel(
    q_in, kb_in, vb_in, kr_in, vr_in, do_in, len_in, fork_in,
    dq_out, dkb_out, dvb_out, dkr_out, dvr_out,
    qs, gs, kbuf, vbuf, pk, pv, rk, rkx, rvx, rvh, rvf,
    exp_own, dp_own, exp_all, dp_all, maxes, total, corr, dq_acc, fork_row, start_row,
    ssem, rsem, lsem,
):
    me = lax.axis_index("mem")
    x, z = me // RING, me % RING
    xn = 1 - x
    zp, zm, z2 = (z + 1) % RING, (z + 3) % RING, (z + 2) % RING

    def at(xi, zi):
        return xi * RING + zi

    def rows(xi, zi, first=0, count=SHARD):
        return pl.ds(pl.multiple_of(at(xi, zi) * SHARD + first, HALF), count)

    def head_cols(h):
        return pl.ds(pl.multiple_of(h * HD, HD), HD)

    right, left, across = at(x, zp), at(x, zm), at(xn, z)

    def copy(h, slot):
        own_k, own_v = kr_in.at[:, head_cols(h)], vr_in.at[:, head_cols(h)]

        def kv(buf, xi, zi, first=0, count=SHARD):
            return buf.at[h, rows(xi, zi, first, count), :]

        def same(buf, xi, zi, to, first=0, count=SHARD):
            ref = kv(buf, xi, zi, first, count)
            return ref, ref, to

        src, dst, to = {
            0: lambda: (own_k, kv(kbuf, x, z), across),
            1: lambda: (own_k, kv(kbuf, x, z), right),
            2: lambda: (own_k, kv(kbuf, x, z), left),
            3: lambda: same(kbuf, xn, z, right),
            4: lambda: same(kbuf, xn, z, left),
            5: lambda: same(kbuf, x, zm, right),
            6: lambda: same(kbuf, xn, zp, left),
            7: lambda: (own_v, kv(vbuf, x, z), across),
            8: lambda: (own_v, kv(vbuf, x, z), right),
            9: lambda: (own_v, kv(vbuf, x, z), left),
            10: lambda: same(vbuf, x, zm, right, 0, HALF),
            11: lambda: same(vbuf, x, zp, left, HALF, HALF),
            12: lambda: same(vbuf, x, zm, across),
            13: lambda: same(vbuf, x, zp, across),
            14: lambda: same(vbuf, x, z2, across, 0, HALF),
            15: lambda: same(vbuf, x, z2, across, HALF, HALF),
            16: lambda: (kv(pk, x, z2), rk.at[h, 0], right),
            17: lambda: (kv(pk, xn, z2), rk.at[h, 1], left),
            18: lambda: (kv(pk, xn, zp), rk.at[h, 2], right),
            19: lambda: (kv(pk, x, zm), rk.at[h, 3], left),
            20: lambda: (kv(pk, x, zp), rk.at[h, 4], right),
            21: lambda: (kv(pk, xn, zm), rk.at[h, 5], left),
            22: lambda: (kv(pk, xn, z), rkx.at[h], across),
            23: lambda: (kv(pv, xn, z2), rvx.at[h, 0], across),
            24: lambda: (kv(pv, xn, zp), rvx.at[h, 1], across),
            25: lambda: (kv(pv, xn, zm), rvx.at[h, 2], across),
            26: lambda: (kv(pv, xn, z), rvx.at[h, 3], across),
            27: lambda: (kv(pv, x, z2, 0, HALF), rvh.at[h, 0], right),
            28: lambda: (kv(pv, x, z2, HALF, HALF), rvh.at[h, 1], left),
            29: lambda: (kv(pv, x, zp), rvf.at[h, 0], right),
            30: lambda: (kv(pv, x, zm), rvf.at[h, 1], left),
        }[slot]()
        return pltpu.make_async_remote_copy(
            src_ref=src, dst_ref=dst,
            send_sem=ssem.at[h, slot], recv_sem=rsem.at[h, slot],
            device_id={"mem": to}, device_id_type=pl.DeviceIdType.MESH,
        )

    def send(h, *slots):
        for slot in slots:
            copy(h, slot).start()

    def arrive(h, *slots):
        for slot in slots:
            copy(h, slot).wait_recv()

    def local(h, which):
        src, buf = ((kr_in, kbuf), (vr_in, vbuf))[which]
        return pltpu.make_async_copy(
            src.at[:, head_cols(h)], buf.at[h, rows(x, z), :], lsem.at[h, which]
        )

    def gather0(h):
        send(h, 0, 8, 9, 1, 2, 7)

    def gather1(h):
        arrive(h, 0, 8, 9, 1)
        send(h, 10, 11, 3, 4, 12, 13, 5)

    def gather2(h):
        arrive(h, 10, 11, 4)
        send(h, 14, 15, 6)

    def gather3(h):
        arrive(h, 2, 3, 5, 6, 7, 12, 13, 14, 15)

    def f32(ref):
        return ref.astype(F32)

    def reduce1(h):
        arrive(h, 23)
        here = rows(x, z2)
        pv[h, here, :] = (f32(pv[h, here, :]) + f32(rvx[h, 0])).astype(BF16)
        send(h, 27, 28)
        arrive(h, 16)
        here = rows(x, zp)
        pk[h, here, :] = (f32(pk[h, here, :]) + f32(rk[h, 0])).astype(BF16)
        send(h, 20)
        arrive(h, 17)
        here = rows(xn, zm)
        pk[h, here, :] = (f32(pk[h, here, :]) + f32(rk[h, 1])).astype(BF16)
        send(h, 21)

    def reduce2(h):
        arrive(h, 24, 25, 27, 28)
        here, rest = rows(x, zp, 0, HALF), rows(x, zp, HALF, HALF)
        pv[h, here, :] = (f32(pv[h, here, :]) + f32(rvx[h, 1, :HALF]) + f32(rvh[h, 0])).astype(BF16)
        pv[h, rest, :] = (f32(pv[h, rest, :]) + f32(rvx[h, 1, HALF:])).astype(BF16)
        send(h, 29)
        here, rest = rows(x, zm, HALF, HALF), rows(x, zm, 0, HALF)
        pv[h, here, :] = (f32(pv[h, here, :]) + f32(rvx[h, 2, HALF:]) + f32(rvh[h, 1])).astype(BF16)
        pv[h, rest, :] = (f32(pv[h, rest, :]) + f32(rvx[h, 2, :HALF])).astype(BF16)
        send(h, 30)
        arrive(h, 18, 21)
        here = rows(xn, z)
        pk[h, here, :] = (f32(pk[h, here, :]) + f32(rk[h, 2]) + f32(rk[h, 5])).astype(BF16)
        send(h, 22)

    def reduce3(h):
        own = rows(x, z)
        arrive(h, 26, 29, 30)
        dvr_out[:, head_cols(h)] = (
            f32(pv[h, own, :]) + f32(rvx[h, 3]) + f32(rvf[h, 0]) + f32(rvf[h, 1])
        ).astype(BF16)
        arrive(h, 19, 20, 22)
        dkr_out[:, head_cols(h)] = (
            f32(pk[h, own, :]) + f32(rk[h, 3]) + f32(rk[h, 4]) + f32(rkx[h])
        ).astype(BF16)

    barrier = pltpu.get_barrier_semaphore()
    for peer in (right, left, across):
        pl.semaphore_signal(
            barrier, inc=1, device_id={"mem": peer}, device_id_type=pl.DeviceIdType.MESH
        )
    for h in range(KVH):
        local(h, 0).start()
        local(h, 1).start()
    pl.semaphore_wait(barrier, 3)
    gather0(0)
    gather0(1)

    lens = [len_in[0, b] for b in range(4)]
    ends = [lens[0], lens[0] + lens[1], lens[0] + lens[1] + lens[2]]
    place = lax.broadcasted_iota(jnp.int32, (1, NQ), 1) % TOK
    fork = jnp.full((1, NQ), fork_in[0, 0], jnp.int32)
    start = jnp.zeros((1, NQ), jnp.int32)
    for b, end in enumerate(ends):
        fork = jnp.where(place >= end, fork_in[0, b + 1], fork)
        start = jnp.where(place >= end, end, start)
    fork_row[...] = fork
    start_row[...] = start

    def lay_out(h, carry):
        for g in range(GROUP):
            cols = pl.ds(pl.multiple_of((h * GROUP + g) * HD, HD), HD)
            qs[h, g * TOK : (g + 1) * TOK, :] = q_in[:, cols]
            gs[h, g * TOK : (g + 1) * TOK, :] = do_in[:, cols]
        return carry

    lax.fori_loop(0, KVH, lay_out, 0)
    gather1(0)
    gather2(0)
    for h in range(KVH):
        local(h, 0).wait()
        local(h, 1).wait()

    order = [
        (xn, z2), (x, z2), (xn, zp), (xn, zm), (xn, z), (x, zp), (x, zm), (x, z),
    ]

    def scores(key, h, lanes):
        return lax.dot_general(key, qs[h, lanes, :], NT, preferred_element_type=F32)

    def grads(value, h, lanes):
        return lax.dot_general(value, gs[h, lanes, :], NT, preferred_element_type=F32)

    lane_tiles = [slice(t, t + LT) for t in range(0, NQ, LT)]

    def first_own(h):
        key, value = kb_in[:, head_cols(h)], vb_in[:, head_cols(h)]
        for lanes in lane_tiles:
            row = lax.broadcasted_iota(jnp.int32, (TOK, LT), 0)
            lane = lax.broadcasted_iota(jnp.int32, (TOK, LT), 1) % TOK
            seen = (row <= lane) & (row >= start_row[:, lanes])
            s = jnp.where(seen, scores(key, h, lanes), NEG)
            top = jnp.max(s, axis=0, keepdims=True)
            e = jnp.exp2(s * C2 - top * C2)
            dp = grads(value, h, lanes)
            total[:, lanes] = jnp.sum(e, axis=0, keepdims=True)
            corr[:, lanes] = jnp.sum(e * dp, axis=0, keepdims=True)
            exp_own[:, lanes] = e
            dp_own[:, lanes] = dp
            maxes[0:1, lanes] = top

    def first_root(h, i):
        xi, zi = order[i]
        here = rows(xi, zi)
        key, value = kbuf[h, here, :], vbuf[h, here, :]
        base = at(xi, zi) * SHARD
        for lanes in lane_tiles:
            row = lax.broadcasted_iota(jnp.int32, (SHARD, LT), 0)
            s = jnp.where(row < fork_row[:, lanes] - base, scores(key, h, lanes), NEG)
            before = maxes[i : i + 1, lanes]
            top = jnp.maximum(before, jnp.max(s, axis=0, keepdims=True))
            shrink = jnp.exp2((before - top) * C2)
            e = jnp.exp2(s * C2 - top * C2)
            dp = grads(value, h, lanes)
            total[:, lanes] = total[:, lanes] * shrink + jnp.sum(e, axis=0, keepdims=True)
            corr[:, lanes] = corr[:, lanes] * shrink + jnp.sum(e * dp, axis=0, keepdims=True)
            exp_all[i, :, lanes] = e
            dp_all[i, :, lanes] = dp
            maxes[i + 1 : i + 2, lanes] = top

    def second(h, key, e_ref, dp_ref, i):
        turned = key.T
        count = key.shape[0]
        dk = jnp.zeros((count, HD), F32)
        dv = jnp.zeros((count, HD), F32)
        for lanes in lane_tiles:
            p = e_ref[:, lanes] * maxes[i : i + 1, lanes]
            ds = (p * (dp_ref[:, lanes] - corr[:, lanes])).astype(BF16)
            dk += jnp.dot(ds, qs[h, lanes, :], preferred_element_type=F32)
            dv += jnp.dot(p.astype(BF16), gs[h, lanes, :], preferred_element_type=F32)
            dq_acc[:, lanes] += jnp.dot(turned, ds, preferred_element_type=F32)
        return (dk * SCALE).astype(BF16), dv.astype(BF16)

    def second_root(h, i):
        here = rows(*order[i])
        dk, dv = second(h, kbuf[h, here, :], exp_all.at[i], dp_all.at[i], i + 1)
        pk[h, here, :] = dk
        pv[h, here, :] = dv

    def one_head(h, carry):
        gather3(h)
        first_own(h)
        first_root(h, 0)
        first_root(h, 1)

        @pl.when(h < KVH - 1)
        def _():
            gather1(h + 1)

        @pl.when(h > 0)
        def _():
            reduce2(h - 1)

        first_root(h, 2)
        first_root(h, 3)

        @pl.when(h < KVH - 2)
        def _():
            gather0(h + 2)

        @pl.when(h < KVH - 1)
        def _():
            gather2(h + 1)

        first_root(h, 4)
        first_root(h, 5)

        @pl.when(h > 0)
        def _():
            reduce3(h - 1)

        first_root(h, 6)
        first_root(h, 7)

        inverse = 1.0 / total[...]
        maxes[...] = jnp.exp2((maxes[...] - maxes[N_MEM : N_MEM + 1, :]) * C2) * inverse
        corr[...] = corr[...] * inverse
        dq_acc[...] = jnp.zeros((HD, NQ), F32)
        second_root(h, 0)
        send(h, 23, 17)
        second_root(h, 1)
        send(h, 16)
        second_root(h, 2)
        send(h, 24, 18)
        second_root(h, 3)
        send(h, 25)
        second_root(h, 4)
        send(h, 26)
        second_root(h, 5)
        second_root(h, 6)
        send(h, 19)
        second_root(h, 7)
        dk, dv = second(h, kb_in[:, head_cols(h)], exp_own, dp_own, 0)
        dkb_out[:, head_cols(h)] = dk
        dvb_out[:, head_cols(h)] = dv
        for g in range(GROUP):
            cols = pl.ds(pl.multiple_of((h * GROUP + g) * HD, HD), HD)
            dq_out[:, cols] = (dq_acc[:, g * TOK : (g + 1) * TOK].T * SCALE).astype(BF16)
        reduce1(h)
        return carry

    lax.fori_loop(0, KVH, one_head, 0)
    reduce2(KVH - 1)
    reduce3(KVH - 1)

    def drain(h, carry):
        for slot in range(SLOTS):
            copy(h, slot).wait_send()
        return carry

    lax.fori_loop(0, KVH, drain, 0)


def per_device(*args):
    vmem, anywhere, smem = (
        pl.BlockSpec(memory_space=space) for space in (pltpu.VMEM, pl.ANY, pltpu.SMEM)
    )
    buf = pltpu.VMEM
    return pl.pallas_call(
        kernel,
        out_shape=(
            jax.ShapeDtypeStruct((TOK, KVH * GROUP * HD), BF16),
            jax.ShapeDtypeStruct((TOK, KVH * HD), BF16),
            jax.ShapeDtypeStruct((TOK, KVH * HD), BF16),
            jax.ShapeDtypeStruct((SHARD, KVH * HD), BF16),
            jax.ShapeDtypeStruct((SHARD, KVH * HD), BF16),
        ),
        in_specs=[vmem, vmem, vmem, anywhere, anywhere, vmem, smem, smem],
        out_specs=(vmem,) * 5,
        scratch_shapes=[
            buf((KVH, NQ, HD), BF16),
            buf((KVH, NQ, HD), BF16),
            buf((KVH, ROOT, HD), BF16),
            buf((KVH, ROOT, HD), BF16),
            buf((KVH, ROOT, HD), BF16),
            buf((KVH, ROOT, HD), BF16),
            buf((KVH, 6, SHARD, HD), BF16),
            buf((KVH, SHARD, HD), BF16),
            buf((KVH, 4, SHARD, HD), BF16),
            buf((KVH, 2, HALF, HD), BF16),
            buf((KVH, 2, SHARD, HD), BF16),
            buf((TOK, NQ), F32),
            buf((TOK, NQ), F32),
            buf((N_MEM, SHARD, NQ), F32),
            buf((N_MEM, SHARD, NQ), F32),
            buf((N_MEM + 1, NQ), F32),
            buf((1, NQ), F32),
            buf((1, NQ), F32),
            buf((HD, NQ), F32),
            buf((1, NQ), jnp.int32),
            buf((1, NQ), jnp.int32),
            pltpu.SemaphoreType.DMA((KVH, SLOTS)),
            pltpu.SemaphoreType.DMA((KVH, SLOTS)),
            pltpu.SemaphoreType.DMA((KVH, 2)),
        ],
        compiler_params=pltpu.CompilerParams(
            collective_id=0, has_side_effects=True, vmem_limit_bytes=56 * 2**20
        ),
        cost_estimate=pl.CostEstimate(
            flops=12 * 10**9, bytes_accessed=6 * 10**6, transcendentals=9 * 10**6
        ),
    )(*args)


def solution(mesh):
    spec = P(("grp", "mem"), None)
    return jax.shard_map(
        per_device,
        mesh=mesh,
        in_specs=(spec,) * 8,
        out_specs=(spec,) * 5,
        check_vma=False,
    )
```

profile of v0, /device:TPU:0, one launch (start us, length us, event | category | flops | bytes accessed | tf_op | source)
XLA Modules:
  0.0 92.1 jit_solution(6165388589486636496)
XLA Ops:
  0.6 86.1 %shard_map.119 = (bf16[128,4096]{1,0:T(8,128)(2,1)}, bf16[128,512]{1,0:T(8,128)(2,1)}, bf16[128,512]{1,0:T(8,128)(2,1)}, bf16[256,512]{1,0:T(8,128)(2,1)}, bf16[256,512]{1,0:T(8,128)(2,1)}) custom-call(bf16[128,4096]{1,0:T(8,128)(2,1)} %q_in.1, bf16[128,512]{1,0:T(8,128)(2,1)} %kb_in.1, bf16[128,512]{1,0:T(8,128)(2,1)} %vb_in.1, bf16[256,512]{1,0:T(8,128)(2,1)} %kr_in.1, ...), custom_call_target="tpu_custom_call" | custom-call | flops 12000000000 | bytes 6000000 | tf_op jit(solution)/shard_map/pallas_call | solution.py:356
  86.7 0.0 copy-start.3
  86.7 0.0 copy-start.2
  86.7 2.3 %copy.18 = bf16[128,4096]{1,0:T(8,128)(2,1)} copy(bf16[128,4096]{1,0:T(8,128)(2,1)} %get-tuple-element.10) | data formatting | bytes 2097152
  89.0 0.0 copy-done.3
  89.0 0.0 copy-start.1
  89.0 0.7 copy.19
  89.7 0.0 copy-done.2
  89.7 0.7 copy.20
  90.4 0.0 copy-done.1
  90.4 0.0 copy-start
  90.4 0.7 copy.21
  91.1 0.3 copy-done
  91.4 0.7 copy.22
Async XLA Ops:
  86.7 2.4 %copy-start.3 = (bf16[128,512]{1,0:T(8,128)(2,1)S(1)}, bf16[128,512]{1,0:T(8,128)(2,1)}, u32[]{:S(2)}) copy-start(bf16[128,512]{1,0:T(8,128)(2,1)} %get-tuple-element.11) | copy-start | bytes 393220
  86.7 3.0 %copy-start.2 = (bf16[128,512]{1,0:T(8,128)(2,1)S(1)}, bf16[128,512]{1,0:T(8,128)(2,1)}, u32[]{:S(2)}) copy-start(bf16[128,512]{1,0:T(8,128)(2,1)} %get-tuple-element.12) | copy-start | bytes 393220
  89.0 1.3 %copy-start.1 = (bf16[256,512]{1,0:T(8,128)(2,1)S(1)}, bf16[256,512]{1,0:T(8,128)(2,1)}, u32[]{:S(2)}) copy-start(bf16[256,512]{1,0:T(8,128)(2,1)} %get-tuple-element.13) | copy-start | bytes 786436
  90.4 1.0 %copy-start = (bf16[256,512]{1,0:T(8,128)(2,1)S(1)}, bf16[256,512]{1,0:T(8,128)(2,1)}, u32[]{:S(2)}) copy-start(bf16[256,512]{1,0:T(8,128)(2,1)} %get-tuple-element.14) | copy-start | bytes 786436
where the time goes:
time: 92.3 us; the launch traced here: 92.1 us
  Pallas kernels  86.1 us (93%)
  local copies, waits for them, and re-layouts  5.4 us (6%)
    pallas_call x1, Pallas kernels, per_device(): pl.pallas_call(kernel, out_shape=(jax.ShapeDtypeStruct((TOK, KVH * GROUP...  86.1 us
    unnamed x13, local copies, waits for them, and re-layouts  5.4 us

commit v1 on v0

v1 whole, which is shorter than its diff:
```python
import functools
import math

import jax
import jax.numpy as jnp
from jax import lax
from jax.experimental import pallas as pl
from jax.experimental.pallas import tpu as pltpu
from jax.sharding import PartitionSpec as P

KVH = 4
GROUP = 8
HD = 128
TOK = 128
NQ = GROUP * TOK
SHARD = 256
HALF = SHARD // 2
N_MEM = 8
RING = 4
ROOT = SHARD * N_MEM
LT = 256
NEG = -1e30
SCALE = 1.0 / math.sqrt(HD)
C2 = SCALE / math.log(2.0)
SLOTS = 34
QUARTER = SHARD // 4
F32 = jnp.float32
BF16 = jnp.bfloat16
NT = (((1,), (1,)), ((), ()))


def kernel(
    q_in, kb_in, vb_in, kr_in, vr_in, do_in, len_in, fork_in,
    dq_out, dkb_out, dvb_out, dkr_out, dvr_out,
    q_vm, do_vm, dq_vm, small_vm, root_vm,
    qs, gs, kbuf, vbuf, pk, pv, rk, rkx, rvx, rvh, rvf, rvq,
    exp_own, dp_own, exp_all, dp_all, maxes, total, corr, dq_acc, fork_row, start_row,
    ssem, rsem, lsem,
):
    me = lax.axis_index("mem")
    x, z = me // RING, me % RING
    xn = 1 - x
    zp, zm, z2 = (z + 1) % RING, (z + 3) % RING, (z + 2) % RING

    def at(xi, zi):
        return xi * RING + zi

    def rows(xi, zi, first=0, count=SHARD):
        return pl.ds(pl.multiple_of(at(xi, zi) * SHARD + first, QUARTER), count)

    def head_cols(h):
        return pl.ds(pl.multiple_of(h * HD, HD), HD)

    right, left, across = at(x, zp), at(x, zm), at(xn, z)

    def copy(h, slot):
        own_k, own_v = kr_in.at[:, head_cols(h)], vr_in.at[:, head_cols(h)]

        def kv(buf, xi, zi, first=0, count=SHARD):
            return buf.at[h, rows(xi, zi, first, count), :]

        def same(buf, xi, zi, to, first=0, count=SHARD):
            ref = kv(buf, xi, zi, first, count)
            return ref, ref, to

        src, dst, to = {
            0: lambda: (own_k, kv(kbuf, x, z), across),
            1: lambda: (own_k, kv(kbuf, x, z), right),
            2: lambda: (own_k, kv(kbuf, x, z), left),
            3: lambda: same(kbuf, xn, z, right),
            4: lambda: same(kbuf, xn, z, left),
            5: lambda: same(kbuf, x, zm, right),
            6: lambda: same(kbuf, xn, zp, left),
            7: lambda: (own_v, kv(vbuf, x, z), across),
            8: lambda: (own_v, kv(vbuf, x, z), right),
            9: lambda: (own_v, kv(vbuf, x, z), left),
            10: lambda: same(vbuf, x, zm, right, 0, HALF),
            11: lambda: same(vbuf, x, zp, left, HALF, HALF),
            12: lambda: same(vbuf, x, zm, across),
            13: lambda: same(vbuf, x, zp, across),
            14: lambda: same(vbuf, x, z2, across, 0, HALF),
            15: lambda: same(vbuf, xn, zm, right, HALF, QUARTER),
            31: lambda: same(vbuf, xn, zp, left, HALF + QUARTER, QUARTER),
            16: lambda: (kv(pk, x, z2), rk.at[h, 0], right),
            17: lambda: (kv(pk, xn, z2), rk.at[h, 1], left),
            18: lambda: (kv(pk, xn, zp), rk.at[h, 2], right),
            19: lambda: (kv(pk, x, zm), rk.at[h, 3], left),
            20: lambda: (kv(pk, x, zp), rk.at[h, 4], right),
            21: lambda: (kv(pk, xn, zm), rk.at[h, 5], left),
            22: lambda: (kv(pk, xn, z), rkx.at[h], across),
            23: lambda: (kv(pv, xn, z2, 0, HALF), rvx.at[h, 0, pl.ds(0, HALF), :], across),
            32: lambda: (kv(pv, xn, z2, HALF, QUARTER), rvq.at[h, 0], right),
            33: lambda: (kv(pv, xn, z2, HALF + QUARTER, QUARTER), rvq.at[h, 1], left),
            24: lambda: (kv(pv, xn, zp), rvx.at[h, 1], across),
            25: lambda: (kv(pv, xn, zm), rvx.at[h, 2], across),
            26: lambda: (kv(pv, xn, z), rvx.at[h, 3], across),
            27: lambda: (kv(pv, x, z2, 0, HALF), rvh.at[h, 0], right),
            28: lambda: (kv(pv, x, z2, HALF, HALF), rvh.at[h, 1], left),
            29: lambda: (kv(pv, x, zp), rvf.at[h, 0], right),
            30: lambda: (kv(pv, x, zm), rvf.at[h, 1], left),
        }[slot]()
        return pltpu.make_async_remote_copy(
            src_ref=src, dst_ref=dst,
            send_sem=ssem.at[h, slot], recv_sem=rsem.at[h, slot],
            device_id={"mem": to}, device_id_type=pl.DeviceIdType.MESH,
        )

    def send(h, *slots):
        for slot in slots:
            copy(h, slot).start()

    def arrive(h, *slots):
        for slot in slots:
            copy(h, slot).wait_recv()

    def wide_cols(h):
        return pl.ds(pl.multiple_of(h * NQ, NQ), NQ)

    def local(h, which):
        thin, wide, own = head_cols(h), wide_cols(h), rows(x, z)
        src, dst = (
            (kr_in.at[:, thin], kbuf.at[h, own, :]),
            (vr_in.at[:, thin], vbuf.at[h, own, :]),
            (q_in.at[:, wide], q_vm.at[:, wide]),
            (do_in.at[:, wide], do_vm.at[:, wide]),
            (dq_vm.at[:, wide], dq_out.at[:, wide]),
            (small_vm.at[0, h], dkb_out.at[:, thin]),
            (small_vm.at[1, h], dvb_out.at[:, thin]),
            (root_vm.at[0, h], dkr_out.at[:, thin]),
            (root_vm.at[1, h], dvr_out.at[:, thin]),
        )[which]
        return pltpu.make_async_copy(src, dst, lsem.at[h, which])

    def gather0(h):
        send(h, 0, 8, 9, 7, 1, 2)

    def gather1(h):
        arrive(h, 0)
        send(h, 3, 4)
        arrive(h, 8)
        send(h, 12, 10)
        arrive(h, 9)
        send(h, 13, 11)
        arrive(h, 1)
        send(h, 5)

    def gather2(h):
        arrive(h, 4)
        send(h, 6)
        arrive(h, 10)
        send(h, 14)
        arrive(h, 12)
        send(h, 15)
        arrive(h, 13)
        send(h, 31)

    def f32(ref):
        return ref.astype(F32)

    def reduce0(h):
        for side, zi, first in ((0, zp, HALF), (1, zm, HALF + QUARTER)):
            arrive(h, 32 + side)
            here = rows(xn, zi, first, QUARTER)
            pv[h, here, :] = (f32(pv[h, here, :]) + f32(rvq[h, side])).astype(BF16)
            send(h, 24 + side)

    def reduce1(h):
        arrive(h, 23)
        here = rows(x, z2, 0, HALF)
        pv[h, here, :] = (f32(pv[h, here, :]) + f32(rvx[h, 0, :HALF])).astype(BF16)
        send(h, 27)
        arrive(h, 16)
        here = rows(x, zp)
        pk[h, here, :] = (f32(pk[h, here, :]) + f32(rk[h, 0])).astype(BF16)
        send(h, 20)
        arrive(h, 17)
        here = rows(xn, zm)
        pk[h, here, :] = (f32(pk[h, here, :]) + f32(rk[h, 1])).astype(BF16)
        send(h, 21)

    def reduce2(h):
        arrive(h, 24, 25, 27, 28)
        here, rest = rows(x, zp, 0, HALF), rows(x, zp, HALF, HALF)
        pv[h, here, :] = (f32(pv[h, here, :]) + f32(rvx[h, 1, :HALF]) + f32(rvh[h, 0])).astype(BF16)
        pv[h, rest, :] = (f32(pv[h, rest, :]) + f32(rvx[h, 1, HALF:])).astype(BF16)
        send(h, 29)
        here, rest = rows(x, zm, HALF, HALF), rows(x, zm, 0, HALF)
        pv[h, here, :] = (f32(pv[h, here, :]) + f32(rvx[h, 2, HALF:]) + f32(rvh[h, 1])).astype(BF16)
        pv[h, rest, :] = (f32(pv[h, rest, :]) + f32(rvx[h, 2, :HALF])).astype(BF16)
        send(h, 30)
        arrive(h, 18, 21)
        here = rows(xn, z)
        pk[h, here, :] = (f32(pk[h, here, :]) + f32(rk[h, 2]) + f32(rk[h, 5])).astype(BF16)
        send(h, 22)

    def reduce3(h):
        own = rows(x, z)
        arrive(h, 26, 29, 30)
        root_vm[1, h] = (
            f32(pv[h, own, :]) + f32(rvx[h, 3]) + f32(rvf[h, 0]) + f32(rvf[h, 1])
        ).astype(BF16)
        arrive(h, 19, 20, 22)
        local(h, 8).start()
        root_vm[0, h] = (
            f32(pk[h, own, :]) + f32(rk[h, 3]) + f32(rk[h, 4]) + f32(rkx[h])
        ).astype(BF16)
        local(h, 7).start()

    barrier = pltpu.get_barrier_semaphore()
    for peer in (right, left, across):
        pl.semaphore_signal(
            barrier, inc=1, device_id={"mem": peer}, device_id_type=pl.DeviceIdType.MESH
        )
    for h in range(KVH):
        for which in range(4):
            local(h, which).start()
    pl.semaphore_wait(barrier, 3)
    gather0(0)
    gather0(1)

    lens = [len_in[0, b] for b in range(4)]
    ends = [lens[0], lens[0] + lens[1], lens[0] + lens[1] + lens[2]]
    place = lax.broadcasted_iota(jnp.int32, (1, NQ), 1) % TOK
    fork = jnp.full((1, NQ), fork_in[0, 0], jnp.int32)
    start = jnp.zeros((1, NQ), jnp.int32)
    for b, end in enumerate(ends):
        fork = jnp.where(place >= end, fork_in[0, b + 1], fork)
        start = jnp.where(place >= end, end, start)
    fork_row[...] = fork
    start_row[...] = start

    def lay_out(h):
        local(h, 2).wait()
        local(h, 3).wait()
        for g in range(GROUP):
            cols = pl.ds(pl.multiple_of((h * GROUP + g) * HD, HD), HD)
            qs[h, g * TOK : (g + 1) * TOK, :] = q_vm[:, cols]
            gs[h, g * TOK : (g + 1) * TOK, :] = do_vm[:, cols]

    order = [
        (x, z), (xn, z), (x, zp), (x, zm), (xn, zp), (xn, zm), (x, z2), (xn, z2),
    ]

    def scores(key, h, lanes):
        return lax.dot_general(key, qs[h, lanes, :], NT, preferred_element_type=F32)

    def grads(value, h, lanes):
        return lax.dot_general(value, gs[h, lanes, :], NT, preferred_element_type=F32)

    lane_tiles = [slice(t, t + LT) for t in range(0, NQ, LT)]

    def first_own(h, par):
        key, value = kb_in[:, head_cols(h)], vb_in[:, head_cols(h)]
        for lanes in lane_tiles:
            row = lax.broadcasted_iota(jnp.int32, (TOK, LT), 0)
            lane = lax.broadcasted_iota(jnp.int32, (TOK, LT), 1) % TOK
            seen = (row <= lane) & (row >= start_row[:, lanes])
            s = jnp.where(seen, scores(key, h, lanes), NEG)
            top = jnp.max(s, axis=0, keepdims=True)
            e = jnp.exp2(s * C2 - top * C2)
            dp = grads(value, h, lanes)
            total[par, :, lanes] = jnp.sum(e, axis=0, keepdims=True)
            corr[par, :, lanes] = jnp.sum(e * dp, axis=0, keepdims=True)
            exp_own[par, :, lanes] = e
            dp_own[par, :, lanes] = dp
            maxes[par, 0:1, lanes] = top

    def first_root(h, par, i, shard):
        here = pl.ds(pl.multiple_of(shard * SHARD, SHARD), SHARD)
        key, value = kbuf[h, here, :], vbuf[h, here, :]
        base = shard * SHARD
        for lanes in lane_tiles:
            row = lax.broadcasted_iota(jnp.int32, (SHARD, LT), 0)
            s = jnp.where(row < fork_row[:, lanes] - base, scores(key, h, lanes), NEG)
            before = maxes[par, pl.ds(i, 1), lanes]
            top = jnp.maximum(before, jnp.max(s, axis=0, keepdims=True))
            shrink = jnp.exp2((before - top) * C2)
            e = jnp.exp2(s * C2 - top * C2)
            dp = grads(value, h, lanes)
            total[par, :, lanes] = total[par, :, lanes] * shrink + jnp.sum(e, axis=0, keepdims=True)
            corr[par, :, lanes] = corr[par, :, lanes] * shrink + jnp.sum(e * dp, axis=0, keepdims=True)
            exp_all[par, i, :, lanes] = e
            dp_all[par, i, :, lanes] = dp
            maxes[par, pl.ds(i + 1, 1), lanes] = top

    def second(h, par, key, e_ref, dp_ref, i):
        turned = key.T
        count = key.shape[0]
        dk = jnp.zeros((count, HD), F32)
        dv = jnp.zeros((count, HD), F32)
        for lanes in lane_tiles:
            p = e_ref[:, lanes] * maxes[par, pl.ds(i, 1), lanes]
            ds = (p * (dp_ref[:, lanes] - corr[par, :, lanes])).astype(BF16)
            dk += jnp.dot(ds, qs[h, lanes, :], preferred_element_type=F32)
            dv += jnp.dot(p.astype(BF16), gs[h, lanes, :], preferred_element_type=F32)
            dq_acc[:, lanes] += jnp.dot(turned, ds, preferred_element_type=F32)
        return (dk * SCALE).astype(BF16), dv.astype(BF16)

    def second_root(h, par, i, shard):
        here = pl.ds(pl.multiple_of(shard * SHARD, SHARD), SHARD)
        dk, dv = second(h, par, kbuf[h, here, :], exp_all.at[par, i], dp_all.at[par, i], i + 1)
        pk[h, here, :] = dk
        pv[h, here, :] = dv

    def when(condition, step, *args):
        @pl.when(condition)
        def _():
            step(*args)

    shards = [at(xi, zi) for xi, zi in order]

    def step(s, carry):
        now, after = s - 1, s
        odd = s % 2
        even = 1 - odd

        @pl.when(s < KVH)
        def _():
            lay_out(after)
            first_own(after, odd)

        @pl.when(s == 0)
        def _():
            for h in range(KVH):
                local(h, 0).wait()
                local(h, 1).wait()
            gather1(0)
            gather1(1)

        when(s == 1, gather0, 3)

        def first_group(far, carry):
            h = s - far
            par = (odd + far) % 2
            when(far == 0, arrive, h, 7)
            when(far == 1, arrive, h, 3)
            for c in range(4):
                if c == 2:

                    @pl.when((far == 0) & (s == 0))
                    def _():
                        gather2(0)
                        gather0(2)

                    when(far == 0, arrive, h, 2)
                    when(far == 1, arrive, h, 5, 11, 6, 14, 15, 31)
                first_root(h, par, far * 4 + c, jnp.where(far == 0, shards[c], shards[4 + c]))
            when((far == 0) & (s == 2), gather2, 2)
            return carry

        lax.fori_loop(jnp.where(s == KVH, 1, 0), jnp.where(s == 0, 1, 2), first_group, 0)

        def second_half():
            h = now
            inverse = 1.0 / total[even]
            maxes[even] = jnp.exp2((maxes[even] - maxes[even, N_MEM : N_MEM + 1, :]) * C2) * inverse
            corr[even] = corr[even] * inverse
            dq_acc[...] = jnp.zeros((HD, NQ), F32)

            def second_group(near, carry):
                for c, (i, j) in enumerate(((7, 2), (6, 3), (4, 1), (5, 0))):
                    second_root(
                        h, even, jnp.where(near == 0, i, j),
                        jnp.where(near == 0, shards[i], shards[j]),
                    )
                    if c == 1:
                        when(near == 0, send, h, 23, 17, 16, 32, 33, 28)
                        when(near == 1, send, h, 19)

                        @pl.when((near == 0) & (s == 2 - 1))
                        def _():
                            gather2(1)
                            gather1(2)

                        when((near == 0) & (s == 3), gather2, 3)
                when(near == 0, send, h, 18)
                when(near == 1, send, h, 26)
                when((near == 0) & (s == 2), gather1, 3)
                return carry

            lax.fori_loop(0, 2, second_group, 0)
            dk, dv = second(h, even, kb_in[:, head_cols(h)], exp_own.at[even], dp_own.at[even], 0)
            small_vm[0, h] = dk
            small_vm[1, h] = dv
            local(h, 5).start()
            local(h, 6).start()
            for g in range(GROUP):
                cols = pl.ds(pl.multiple_of((h * GROUP + g) * HD, HD), HD)
                dq_vm[:, cols] = (dq_acc[:, g * TOK : (g + 1) * TOK].T * SCALE).astype(BF16)
            local(h, 4).start()
            reduce0(h)
            reduce1(h)

        when(s > 0, second_half)
        when(s > 1, reduce2, s - 2)
        when(s > 2, reduce3, s - 3)
        return carry

    lax.fori_loop(0, KVH + 1, step, 0)
    reduce2(KVH - 1)
    reduce3(KVH - 2)
    reduce3(KVH - 1)

    def drain(h, carry):
        for slot in range(SLOTS):
            copy(h, slot).wait_send()
        for which in range(4, 9):
            local(h, which).wait()
        return carry

    lax.fori_loop(0, KVH, drain, 0)


def hand_over(dq, dkb, dvb, dkr, dvr, dq_out, dkb_out, dvb_out, dkr_out, dvr_out, *rest):
    *held, came, gone = rest
    srcs, dsts = (dq, dkb, dvb, dkr, dvr), (dq_out, dkb_out, dvb_out, dkr_out, dvr_out)
    ins = [pltpu.make_async_copy(a, b, came.at[i]) for i, (a, b) in enumerate(zip(srcs, held))]
    outs = [pltpu.make_async_copy(a, b, gone.at[i]) for i, (a, b) in enumerate(zip(held, dsts))]
    for one in ins:
        one.start()
    for one, other in zip(ins, outs):
        one.wait()
        other.start()
    for other in outs:
        other.wait()


def per_device(*args):
    vmem, anywhere, smem = (
        pl.BlockSpec(memory_space=space) for space in (pltpu.VMEM, pl.ANY, pltpu.SMEM)
    )
    buf = pltpu.VMEM
    outs = pl.pallas_call(
        kernel,
        out_shape=(
            jax.ShapeDtypeStruct((TOK, KVH * GROUP * HD), BF16),
            jax.ShapeDtypeStruct((TOK, KVH * HD), BF16),
            jax.ShapeDtypeStruct((TOK, KVH * HD), BF16),
            jax.ShapeDtypeStruct((SHARD, KVH * HD), BF16),
            jax.ShapeDtypeStruct((SHARD, KVH * HD), BF16),
        ),
        in_specs=[anywhere, vmem, vmem, anywhere, anywhere, anywhere, smem, smem],
        out_specs=(anywhere,) * 5,
        scratch_shapes=[
            buf((TOK, KVH * NQ), BF16),
            buf((TOK, KVH * NQ), BF16),
            buf((TOK, KVH * NQ), BF16),
            buf((2, KVH, TOK, HD), BF16),
            buf((2, KVH, SHARD, HD), BF16),
            buf((KVH, NQ, HD), BF16),
            buf((KVH, NQ, HD), BF16),
            buf((KVH, ROOT, HD), BF16),
            buf((KVH, ROOT, HD), BF16),
            buf((KVH, ROOT, HD), BF16),
            buf((KVH, ROOT, HD), BF16),
            buf((KVH, 6, SHARD, HD), BF16),
            buf((KVH, SHARD, HD), BF16),
            buf((KVH, 4, SHARD, HD), BF16),
            buf((KVH, 2, HALF, HD), BF16),
            buf((KVH, 2, SHARD, HD), BF16),
            buf((KVH, 2, QUARTER, HD), BF16),
            buf((2, TOK, NQ), F32),
            buf((2, TOK, NQ), F32),
            buf((2, N_MEM, SHARD, NQ), F32),
            buf((2, N_MEM, SHARD, NQ), F32),
            buf((2, N_MEM + 1, NQ), F32),
            buf((2, 1, NQ), F32),
            buf((2, 1, NQ), F32),
            buf((HD, NQ), F32),
            buf((1, NQ), jnp.int32),
            buf((1, NQ), jnp.int32),
            pltpu.SemaphoreType.DMA((KVH, SLOTS)),
            pltpu.SemaphoreType.DMA((KVH, SLOTS)),
            pltpu.SemaphoreType.DMA((KVH, 9)),
        ],
        compiler_params=pltpu.CompilerParams(
            collective_id=0, has_side_effects=True, vmem_limit_bytes=60 * 2**20
        ),
        cost_estimate=pl.CostEstimate(
            flops=12 * 10**9, bytes_accessed=6 * 10**6, transcendentals=9 * 10**6
        ),
    )(*args)
    return pl.pallas_call(
        hand_over,
        out_shape=tuple(jax.ShapeDtypeStruct(out.shape, out.dtype) for out in outs),
        in_specs=[anywhere] * 5,
        out_specs=(anywhere,) * 5,
        scratch_shapes=[pltpu.VMEM(out.shape, out.dtype) for out in outs]
        + [pltpu.SemaphoreType.DMA((5,))] * 2,
    )(*outs)


def solution(mesh):
    spec = P(("grp", "mem"), None)
    return jax.shard_map(
        per_device,
        mesh=mesh,
        in_specs=(spec,) * 8,
        out_specs=(spec,) * 5,
        check_vma=False,
    )
```

time: 92.3 us -> 73.4 us (0.80)
  Pallas kernels: 86.1 us -> 72.6 us
  local copies, waits for them, and re-layouts: 5.4 us -> 0 us
    pallas_call x1, Pallas kernels: 86.1 us -> 70.1 us  [per_device(): pl.pallas_call(kernel, out_shape=(jax.ShapeDtypeStruct((TOK, KVH * GROUP...]
    unnamed x13 -> x0, local copies, waits for them, and re-layouts: 5.4 us -> none
    pallas_call x0 -> x1, Pallas kernels: none -> 2.53 us  [per_device(): pl.pallas_call(hand_over, out_shape=tuple((jax.ShapeDtypeStruct(out.shape...]
where the time goes in v1:
time: 73.4 us; the launch traced here: 73.2 us
  Pallas kernels  72.6 us (99%)
    pallas_call x1, Pallas kernels, per_device(): pl.pallas_call(kernel, out_shape=(jax.ShapeDtypeStruct((TOK, KVH * GROUP...  70.1 us
    pallas_call x1, Pallas kernels, per_device(): pl.pallas_call(hand_over, out_shape=tuple((jax.ShapeDtypeStruct(out.shape...  2.53 us

profile of v1, /device:TPU:0, one launch (start us, length us, event | category | flops | bytes accessed | tf_op | source)
XLA Modules:
  0.0 73.2 jit_solution(10602260860755506034)
XLA Ops:
  0.6 70.1 %shard_map.119 = (bf16[128,4096]{1,0:T(8,128)(2,1)}, bf16[128,512]{1,0:T(8,128)(2,1)}, bf16[128,512]{1,0:T(8,128)(2,1)}, bf16[256,512]{1,0:T(8,128)(2,1)}, bf16[256,512]{1,0:T(8,128)(2,1)}) custom-call(bf16[128,4096]{1,0:T(8,128)(2,1)} %q_in.1, bf16[128,512]{1,0:T(8,128)(2,1)} %kb_in.1, bf16[128,512]{1,0:T(8,128)(2,1)} %vb_in.1, bf16[256,512]{1,0:T(8,128)(2,1)} %kr_in.1, ...), custom_call_target="tpu_custom_call" | custom-call | flops 12000000000 | bytes 6000000 | tf_op jit(solution)/shard_map/pallas_call | solution.py:433
  70.7 2.5 %shard_map.120 = (bf16[128,4096]{1,0:T(8,128)(2,1)}, bf16[128,512]{1,0:T(8,128)(2,1)}, bf16[128,512]{1,0:T(8,128)(2,1)}, bf16[256,512]{1,0:T(8,128)(2,1)}, bf16[256,512]{1,0:T(8,128)(2,1)}) custom-call(bf16[128,4096]{1,0:T(8,128)(2,1)} %get-tuple-element.10.dq, bf16[128,512]{1,0:T(8,128)(2,1)} %get-tuple-element.11.dkb, ...), custom_call_target="tpu_custom_call" | custom-call | tf_op jit(solution)/shard_map/pallas_call | solution.py:483

commit v2 on v1

--- a/solution.py
+++ b/solution.py
@@ -23,6 +23,36 @@
 SCALE = 1.0 / math.sqrt(HD)
 C2 = SCALE / math.log(2.0)
 SLOTS = 34
+START, OWN, NEAR_A, NEAR_B, FAR_A, FAR_B, BACK_A, BACK_B, BACK_C, BACK_D, DONE = range(11)
+PLAN = {
+    (START, 0): [(1, 0), (0, 0), (3, 0), (1, 1), (3, 1), (2, 1), (2, 0), (5, 0), (4, 0)],
+    (OWN, 0): [(7, 0), (6, 0), (0, 1), (1, 2)],
+    (NEAR_A, 0): [(6, 1)],
+    (NEAR_B, 0): [(8, 0), (9, 0), (0, 2), (5, 1), (10, 0), (0, 3), (11, 0), (2, 2), (4, 1)],
+    (OWN, 1): [(1, 3)],
+    (NEAR_A, 1): [(7, 1), (11, 1)],
+    (NEAR_B, 1): [(6, 2), (3, 2)],
+    (FAR_B, 0): [(9, 1), (4, 2), (8, 1)],
+    (BACK_A, 0): [(10, 1), (5, 2)],
+    (OWN, 2): [(2, 3), (3, 3), (6, 3)],
+    (NEAR_A, 2): [(4, 3), (7, 2), (8, 2)],
+    (FAR_A, 1): [(5, 3), (11, 2), (10, 2)],
+    (BACK_A, 1): [(9, 2)],
+    (BACK_D, 1): [(11, 3), (7, 3)],
+    (OWN, 3): [(15, 0)],
+    (NEAR_A, 3): [(12, 0), (13, 0), (16, 0), (9, 3)],
+    (FAR_B, 2): [(14, 0), (8, 3), (10, 3), (12, 1)],
+    (BACK_B, 2): [(13, 1)],
+    (BACK_C, 2): [(16, 1)],
+    (BACK_D, 2): [(17, 0), (14, 1)],
+    (FAR_A, 3): [(15, 2), (19, 0)],
+    (FAR_B, 3): [(16, 2), (12, 2)],
+    (BACK_A, 3): [(13, 2), (14, 2), (18, 1), (15, 1)],
+    (BACK_B, 3): [(19, 1), (14, 3), (17, 1), (18, 0), (12, 3), (13, 3), (21, 0), (16, 3)],
+    (BACK_C, 3): [(17, 2)],
+    (BACK_D, 3): [(15, 3), (18, 2), (19, 2), (17, 3), (20, 0), (21, 1), (19, 3), (18, 3)],
+    (DONE, 3): [(20, 2), (21, 2), (20, 1), (21, 3), (20, 3)],
+}
 QUARTER = SHARD // 4
 F32 = jnp.float32
 BF16 = jnp.bfloat16
@@ -131,80 +161,98 @@
         )[which]
         return pltpu.make_async_copy(src, dst, lsem.at[h, which])
 
-    def gather0(h):
-        send(h, 0, 8, 9, 7, 1, 2)
-
-    def gather1(h):
-        arrive(h, 0)
-        send(h, 3, 4)
-        arrive(h, 8)
-        send(h, 12, 10)
-        arrive(h, 9)
-        send(h, 13, 11)
-        arrive(h, 1)
-        send(h, 5)
-
-    def gather2(h):
-        arrive(h, 4)
-        send(h, 6)
-        arrive(h, 10)
-        send(h, 14)
-        arrive(h, 12)
-        send(h, 15)
-        arrive(h, 13)
-        send(h, 31)
-
     def f32(ref):
         return ref.astype(F32)
 
-    def reduce0(h):
-        for side, zi, first in ((0, zp, HALF), (1, zm, HALF + QUARTER)):
-            arrive(h, 32 + side)
-            here = rows(xn, zi, first, QUARTER)
-            pv[h, here, :] = (f32(pv[h, here, :]) + f32(rvq[h, side])).astype(BF16)
-            send(h, 24 + side)
-
-    def reduce1(h):
+    def plus(buf, h, here, *terms):
+        total_here = f32(buf[h, here, :])
+        for term in terms:
+            total_here = total_here + f32(term)
+        buf[h, here, :] = total_here.astype(BF16)
+
+    def pass_on(h, waits, sends):
+        arrive(h, *waits)
+        send(h, *sends)
+
+    def value_side(h, side):
+        arrive(h, 32 + side)
+        zi, first = ((zp, HALF), (zm, HALF + QUARTER))[side]
+        plus(pv, h, rows(xn, zi, first, QUARTER), rvq[h, side])
+        send(h, 24 + side)
+
+    def value_half(h):
         arrive(h, 23)
-        here = rows(x, z2, 0, HALF)
-        pv[h, here, :] = (f32(pv[h, here, :]) + f32(rvx[h, 0, :HALF])).astype(BF16)
+        plus(pv, h, rows(x, z2, 0, HALF), rvx[h, 0, :HALF])
         send(h, 27)
-        arrive(h, 16)
-        here = rows(x, zp)
-        pk[h, here, :] = (f32(pk[h, here, :]) + f32(rk[h, 0])).astype(BF16)
-        send(h, 20)
-        arrive(h, 17)
-        here = rows(xn, zm)
-        pk[h, here, :] = (f32(pk[h, here, :]) + f32(rk[h, 1])).astype(BF16)
-        send(h, 21)
-
-    def reduce2(h):
-        arrive(h, 24, 25, 27, 28)
-        here, rest = rows(x, zp, 0, HALF), rows(x, zp, HALF, HALF)
-        pv[h, here, :] = (f32(pv[h, here, :]) + f32(rvx[h, 1, :HALF]) + f32(rvh[h, 0])).astype(BF16)
-        pv[h, rest, :] = (f32(pv[h, rest, :]) + f32(rvx[h, 1, HALF:])).astype(BF16)
-        send(h, 29)
-        here, rest = rows(x, zm, HALF, HALF), rows(x, zm, 0, HALF)
-        pv[h, here, :] = (f32(pv[h, here, :]) + f32(rvx[h, 2, HALF:]) + f32(rvh[h, 1])).astype(BF16)
-        pv[h, rest, :] = (f32(pv[h, rest, :]) + f32(rvx[h, 2, :HALF])).astype(BF16)
-        send(h, 30)
+
+    def key_side(h, side):
+        arrive(h, 16 + side)
+        plus(pk, h, (rows(x, zp), rows(xn, zm))[side], rk[h, side])
+        send(h, 20 + side)
+
+    def value_block(h, side):
+        arrive(h, 24 + side, 27 + side)
+        zi = (zp, zm)[side]
+        first, other = ((0, HALF), (HALF, 0))[side]
+        plus(pv, h, rows(x, zi, first, HALF), rvx[h, 1 + side, first : first + HALF], rvh[h, side])
+        plus(pv, h, rows(x, zi, other, HALF), rvx[h, 1 + side, other : other + HALF])
+        send(h, 29 + side)
+
+    def key_across(h):
         arrive(h, 18, 21)
-        here = rows(xn, z)
-        pk[h, here, :] = (f32(pk[h, here, :]) + f32(rk[h, 2]) + f32(rk[h, 5])).astype(BF16)
+        plus(pk, h, rows(xn, z), rk[h, 2], rk[h, 5])
         send(h, 22)
 
-    def reduce3(h):
-        own = rows(x, z)
+    def value_out(h):
         arrive(h, 26, 29, 30)
         root_vm[1, h] = (
-            f32(pv[h, own, :]) + f32(rvx[h, 3]) + f32(rvf[h, 0]) + f32(rvf[h, 1])
+            f32(pv[h, rows(x, z), :]) + f32(rvx[h, 3]) + f32(rvf[h, 0]) + f32(rvf[h, 1])
         ).astype(BF16)
+        local(h, 8).start()
+
+    def key_out(h):
         arrive(h, 19, 20, 22)
-        local(h, 8).start()
         root_vm[0, h] = (
-            f32(pk[h, own, :]) + f32(rk[h, 3]) + f32(rk[h, 4]) + f32(rkx[h])
+            f32(pk[h, rows(x, z), :]) + f32(rk[h, 3]) + f32(rk[h, 4]) + f32(rkx[h])
         ).astype(BF16)
         local(h, 7).start()
+
+    steps = [
+        lambda h: send(h, 0),
+        lambda h: send(h, 8, 9),
+        lambda h: send(h, 7),
+        lambda h: send(h, 1, 2),
+        lambda h: pass_on(h, (0,), (3, 4)),
+        lambda h: pass_on(h, (8,), (12, 10)),
+        lambda h: pass_on(h, (9,), (13, 11)),
+        lambda h: pass_on(h, (1,), (5,)),
+        lambda h: pass_on(h, (4,), (6,)),
+        lambda h: pass_on(h, (10,), (14,)),
+        lambda h: pass_on(h, (12,), (15,)),
+        lambda h: pass_on(h, (13,), (31,)),
+        lambda h: value_side(h, 0),
+        lambda h: value_side(h, 1),
+        value_half,
+        lambda h: key_side(h, 0),
+        lambda h: key_side(h, 1),
+        lambda h: value_block(h, 0),
+        lambda h: value_block(h, 1),
+        key_across,
+        value_out,
+        key_out,
+    ]
+
+    def run(piece, head):
+        for number, h in PLAN.get((piece, head), ()):
+            steps[number](h)
+
+    def run_when(piece, head, guard=None):
+        for h in range(KVH):
+            if (piece, h) in PLAN:
+
+                @pl.when(head == h if guard is None else (head == h) & guard)
+                def _():
+                    run(piece, h)
 
     barrier = pltpu.get_barrier_semaphore()
     for peer in (right, left, across):
@@ -214,10 +262,6 @@
     for h in range(KVH):
         for which in range(4):
             local(h, which).start()
-    pl.semaphore_wait(barrier, 3)
-    gather0(0)
-    gather0(1)
-
     lens = [len_in[0, b] for b in range(4)]
     ends = [lens[0], lens[0] + lens[1], lens[0] + lens[1] + lens[2]]
     place = lax.broadcasted_iota(jnp.int32, (1, NQ), 1) % TOK
@@ -236,6 +280,13 @@
             cols = pl.ds(pl.multiple_of((h * GROUP + g) * HD, HD), HD)
             qs[h, g * TOK : (g + 1) * TOK, :] = q_vm[:, cols]
             gs[h, g * TOK : (g + 1) * TOK, :] = do_vm[:, cols]
+
+    lay_out(0)
+    for h in range(KVH):
+        local(h, 0).wait()
+        local(h, 1).wait()
+    pl.semaphore_wait(barrier, 3)
+    run(START, 0)
 
     order = [
         (x, z), (xn, z), (x, zp), (x, zm), (xn, zp), (xn, zm), (x, z2), (xn, z2),
@@ -316,18 +367,13 @@
 
         @pl.when(s < KVH)
         def _():
-            lay_out(after)
             first_own(after, odd)
 
-        @pl.when(s == 0)
+        @pl.when(s < KVH - 1)
         def _():
-            for h in range(KVH):
-                local(h, 0).wait()
-                local(h, 1).wait()
-            gather1(0)
-            gather1(1)
-
-        when(s == 1, gather0, 3)
+            lay_out(s + 1)
+
+        run_when(OWN, s)
 
         def first_group(far, carry):
             h = s - far
@@ -337,15 +383,13 @@
             for c in range(4):
                 if c == 2:
 
-                    @pl.when((far == 0) & (s == 0))
-                    def _():
-                        gather2(0)
-                        gather0(2)
-
+                    run_when(NEAR_A, h, far == 0)
+                    run_when(FAR_A, h, far == 1)
                     when(far == 0, arrive, h, 2)
                     when(far == 1, arrive, h, 5, 11, 6, 14, 15, 31)
                 first_root(h, par, far * 4 + c, jnp.where(far == 0, shards[c], shards[4 + c]))
-            when((far == 0) & (s == 2), gather2, 2)
+            run_when(NEAR_B, h, far == 0)
+            run_when(FAR_B, h, far == 1)
             return carry
 
         lax.fori_loop(jnp.where(s == KVH, 1, 0), jnp.where(s == 0, 1, 2), first_group, 0)
@@ -367,15 +411,12 @@
                         when(near == 0, send, h, 23, 17, 16, 32, 33, 28)
                         when(near == 1, send, h, 19)
 
-                        @pl.when((near == 0) & (s == 2 - 1))
-                        def _():
-                            gather2(1)
-                            gather1(2)
-
-                        when((near == 0) & (s == 3), gather2, 3)
+                        run_when(BACK_A, h, near == 0)
+                        run_when(BACK_C, h, near == 1)
                 when(near == 0, send, h, 18)
                 when(near == 1, send, h, 26)
-                when((near == 0) & (s == 2), gather1, 3)
+                run_when(BACK_B, h, near == 0)
+                run_when(BACK_D, h, near == 1)
                 return carry
 
             lax.fori_loop(0, 2, second_group, 0)
@@ -388,18 +429,12 @@
                 cols = pl.ds(pl.multiple_of((h * GROUP + g) * HD, HD), HD)
                 dq_vm[:, cols] = (dq_acc[:, g * TOK : (g + 1) * TOK].T * SCALE).astype(BF16)
             local(h, 4).start()
-            reduce0(h)
-            reduce1(h)
+            run_when(DONE, h)
 
         when(s > 0, second_half)
-        when(s > 1, reduce2, s - 2)
-        when(s > 2, reduce3, s - 3)
         return carry
 
     lax.fori_loop(0, KVH + 1, step, 0)
-    reduce2(KVH - 1)
-    reduce3(KVH - 2)
-    reduce3(KVH - 1)
 
     def drain(h, carry):
         for slot in range(SLOTS):
@@ -411,18 +446,13 @@
     lax.fori_loop(0, KVH, drain, 0)
 
 
-def hand_over(dq, dkb, dvb, dkr, dvr, dq_out, dkb_out, dvb_out, dkr_out, dvr_out, *rest):
-    *held, came, gone = rest
+def hand_over(dq, dkb, dvb, dkr, dvr, dq_out, dkb_out, dvb_out, dkr_out, dvr_out, gone):
     srcs, dsts = (dq, dkb, dvb, dkr, dvr), (dq_out, dkb_out, dvb_out, dkr_out, dvr_out)
-    ins = [pltpu.make_async_copy(a, b, came.at[i]) for i, (a, b) in enumerate(zip(srcs, held))]
-    outs = [pltpu.make_async_copy(a, b, gone.at[i]) for i, (a, b) in enumerate(zip(held, dsts))]
-    for one in ins:
+    outs = [pltpu.make_async_copy(a, b, gone.at[i]) for i, (a, b) in enumerate(zip(srcs, dsts))]
+    for one in outs:
         one.start()
-    for one, other in zip(ins, outs):
+    for one in outs:
         one.wait()
-        other.start()
-    for other in outs:
-        other.wait()
 
 
 def per_device(*args):
@@ -433,11 +463,11 @@
     outs = pl.pallas_call(
         kernel,
         out_shape=(
-            jax.ShapeDtypeStruct((TOK, KVH * GROUP * HD), BF16),
-            jax.ShapeDtypeStruct((TOK, KVH * HD), BF16),
-            jax.ShapeDtypeStruct((TOK, KVH * HD), BF16),
-            jax.ShapeDtypeStruct((SHARD, KVH * HD), BF16),
-            jax.ShapeDtypeStruct((SHARD, KVH * HD), BF16),
+            buf((TOK, KVH * GROUP * HD), BF16),
+            buf((TOK, KVH * HD), BF16),
+            buf((TOK, KVH * HD), BF16),
+            buf((SHARD, KVH * HD), BF16),
+            buf((SHARD, KVH * HD), BF16),
         ),
         in_specs=[anywhere, vmem, vmem, anywhere, anywhere, anywhere, smem, smem],
         out_specs=(anywhere,) * 5,
@@ -485,9 +515,8 @@
         out_shape=tuple(jax.ShapeDtypeStruct(out.shape, out.dtype) for out in outs),
         in_specs=[anywhere] * 5,
         out_specs=(anywhere,) * 5,
-        scratch_shapes=[pltpu.VMEM(out.shape, out.dtype) for out in outs]
-        + [pltpu.SemaphoreType.DMA((5,))] * 2,
-    )(*outs)
+        scratch_shapes=[pltpu.SemaphoreType.DMA((5,))],
+    )(*[pltpu.with_memory_space_constraint(out, pltpu.VMEM) for out in outs])
 
 
 def solution(mesh):

time: 73.4 us -> 67.9 us (0.925)
  Pallas kernels: 72.6 us -> 67.1 us
    pallas_call x1, Pallas kernels: 70.1 us -> 65.9 us  [per_device(): pl.pallas_call(kernel, out_shape=(buf((TOK, KVH * GROUP * HD), BF16), buf...]
    pallas_call x1, Pallas kernels: 2.53 us -> 1.27 us  [per_device(): pl.pallas_call(hand_over, out_shape=tuple((jax.ShapeDtypeStruct(out.shape...]
where the time goes in v2:
time: 67.9 us; the launch traced here: 67.8 us
  Pallas kernels  67.1 us (99%)
    pallas_call x1, Pallas kernels, per_device(): pl.pallas_call(kernel, out_shape=(buf((TOK, KVH * GROUP * HD), BF16), buf...  65.9 us

profile of v2, /device:TPU:0, one launch (start us, length us, event | category | flops | bytes accessed | tf_op | source)
XLA Modules:
  0.0 67.8 jit_solution(2696168845703568417)
XLA Ops:
  0.6 65.9 %shard_map.119 = (bf16[128,4096]{1,0:T(8,128)(2,1)S(1)}, bf16[128,512]{1,0:T(8,128)(2,1)S(1)}, bf16[128,512]{1,0:T(8,128)(2,1)S(1)}, bf16[256,512]{1,0:T(8,128)(2,1)S(1)}, bf16[256,512]{1,0:T(8,128)(2,1)S(1)}) custom-call(bf16[128,4096]{1,0:T(8,128)(2,1)} %q_in.1, bf16[128,512]{1,0:T(8,128)(2,1)} %kb_in.1, bf16[128,512]{1,0:T(8,128)(2,1)} %vb_in.1, ...), custom_call_target="tpu_custom_call" | custom-call | flops 12000000000 | bytes 6000000 | tf_op jit(solution)/shard_map/pallas_call | solution.py:463
  66.5 1.3 %shard_map.120 = (bf16[128,4096]{1,0:T(8,128)(2,1)}, bf16[128,512]{1,0:T(8,128)(2,1)}, bf16[128,512]{1,0:T(8,128)(2,1)}, bf16[256,512]{1,0:T(8,128)(2,1)}, bf16[256,512]{1,0:T(8,128)(2,1)}) custom-call(bf16[128,4096]{1,0:T(8,128)(2,1)S(1)} %get-tuple-element.10.dq, bf16[128,512]{1,0:T(8,128)(2,1)S(1)} %get-tuple-element.11.dkb, ...), custom_call_target="tpu_custom_call" | custom-call | tf_op jit(solution)/shard_map/pallas_call | solution.py:513

commit v3 on v2

--- a/solution.py
+++ b/solution.py
@@ -14,7 +14,10 @@
 TOK = 128
 NQ = GROUP * TOK
 SHARD = 256
-HALF = SHARD // 2
+MAIN = 160
+SIDES = (16, 80)
+REST = SHARD - MAIN
+ROW_TILE = 16
 N_MEM = 8
 RING = 4
 ROOT = SHARD * N_MEM
@@ -25,35 +28,30 @@
 SLOTS = 34
 START, OWN, NEAR_A, NEAR_B, FAR_A, FAR_B, BACK_A, BACK_B, BACK_C, BACK_D, DONE = range(11)
 PLAN = {
-    (START, 0): [(1, 0), (0, 0), (3, 0), (1, 1), (3, 1), (2, 1), (2, 0), (5, 0), (4, 0)],
-    (OWN, 0): [(7, 0), (6, 0), (0, 1), (1, 2)],
-    (NEAR_A, 0): [(6, 1)],
-    (NEAR_B, 0): [(8, 0), (9, 0), (0, 2), (5, 1), (10, 0), (0, 3), (11, 0), (2, 2), (4, 1)],
-    (OWN, 1): [(1, 3)],
-    (NEAR_A, 1): [(7, 1), (11, 1)],
-    (NEAR_B, 1): [(6, 2), (3, 2)],
-    (FAR_B, 0): [(9, 1), (4, 2), (8, 1)],
-    (BACK_A, 0): [(10, 1), (5, 2)],
-    (OWN, 2): [(2, 3), (3, 3), (6, 3)],
-    (NEAR_A, 2): [(4, 3), (7, 2), (8, 2)],
-    (FAR_A, 1): [(5, 3), (11, 2), (10, 2)],
-    (BACK_A, 1): [(9, 2)],
-    (BACK_D, 1): [(11, 3), (7, 3)],
-    (OWN, 3): [(15, 0)],
-    (NEAR_A, 3): [(12, 0), (13, 0), (16, 0), (9, 3)],
-    (FAR_B, 2): [(14, 0), (8, 3), (10, 3), (12, 1)],
-    (BACK_B, 2): [(13, 1)],
-    (BACK_C, 2): [(16, 1)],
-    (BACK_D, 2): [(17, 0), (14, 1)],
-    (FAR_A, 3): [(15, 2), (19, 0)],
-    (FAR_B, 3): [(16, 2), (12, 2)],
-    (BACK_A, 3): [(13, 2), (14, 2), (18, 1), (15, 1)],
-    (BACK_B, 3): [(19, 1), (14, 3), (17, 1), (18, 0), (12, 3), (13, 3), (21, 0), (16, 3)],
-    (BACK_C, 3): [(17, 2)],
-    (BACK_D, 3): [(15, 3), (18, 2), (19, 2), (17, 3), (20, 0), (21, 1), (19, 3), (18, 3)],
-    (DONE, 3): [(20, 2), (21, 2), (20, 1), (21, 3), (20, 3)],
+    (START, 0): [(1, 0), (0, 0), (3, 0), (1, 1), (2, 0), (0, 1), (5, 0), (4, 0), (6, 0)],
+    (OWN, 0): [(2, 1), (3, 1), (4, 1)],
+    (NEAR_A, 0): [(9, 0), (8, 0), (7, 0), (0, 2), (10, 0), (5, 1), (11, 0), (1, 2), (1, 3), (3, 2), (6, 1), (0, 3)],
+    (NEAR_B, 0): [(7, 1), (2, 2)],
+    (NEAR_B, 1): [(8, 1)],
+    (FAR_B, 0): [(10, 1)],
+    (BACK_B, 0): [(11, 1), (5, 2), (4, 2), (9, 1), (3, 3)],
+    (BACK_C, 0): [(6, 2)],
+    (BACK_D, 0): [(7, 2), (5, 3)],
+    (NEAR_A, 2): [(2, 3), (4, 3)],
+    (FAR_B, 1): [(10, 2), (12, 0), (11, 2), (9, 2), (8, 2)],
+    (BACK_B, 1): [(6, 3), (16, 0)],
+    (BACK_C, 1): [(7, 3), (13, 0)],
+    (NEAR_A, 3): [(14, 0)],
+    (FAR_B, 2): [(13, 1), (9, 3), (15, 1), (10, 3), (12, 1), (11, 3), (8, 3)],
+    (BACK_B, 2): [(19, 0)],
+    (BACK_C, 2): [(16, 1), (14, 1), (17, 0)],
+    (DONE, 2): [(15, 0)],
+    (FAR_B, 3): [(12, 2), (18, 1)],
+    (BACK_B, 3): [(14, 2), (13, 2), (15, 2)],
+    (BACK_C, 3): [(16, 2), (19, 1), (12, 3), (16, 3), (14, 3), (15, 3), (13, 3), (21, 0)],
+    (BACK_D, 3): [(21, 1), (17, 2), (17, 1), (18, 0), (19, 2), (18, 2), (17, 3)],
+    (DONE, 3): [(19, 3), (18, 3), (22, 3), (20, 2), (20, 1), (20, 0), (21, 2), (21, 3), (20, 3)],
 }
-QUARTER = SHARD // 4
 F32 = jnp.float32
 BF16 = jnp.bfloat16
 NT = (((1,), (1,)), ((), ()))
@@ -62,7 +60,7 @@
 def kernel(
     q_in, kb_in, vb_in, kr_in, vr_in, do_in, len_in, fork_in,
     dq_out, dkb_out, dvb_out, dkr_out, dvr_out,
-    q_vm, do_vm, dq_vm, small_vm, root_vm,
+    q_vm, do_vm,
     qs, gs, kbuf, vbuf, pk, pv, rk, rkx, rvx, rvh, rvf, rvq,
     exp_own, dp_own, exp_all, dp_all, maxes, total, corr, dq_acc, fork_row, start_row,
     ssem, rsem, lsem,
@@ -76,7 +74,7 @@
         return xi * RING + zi
 
     def rows(xi, zi, first=0, count=SHARD):
-        return pl.ds(pl.multiple_of(at(xi, zi) * SHARD + first, QUARTER), count)
+        return pl.ds(pl.multiple_of(at(xi, zi) * SHARD + first, ROW_TILE), count)
 
     def head_cols(h):
         return pl.ds(pl.multiple_of(h * HD, HD), HD)
@@ -104,13 +102,13 @@
             7: lambda: (own_v, kv(vbuf, x, z), across),
             8: lambda: (own_v, kv(vbuf, x, z), right),
             9: lambda: (own_v, kv(vbuf, x, z), left),
-            10: lambda: same(vbuf, x, zm, right, 0, HALF),
-            11: lambda: same(vbuf, x, zp, left, HALF, HALF),
+            10: lambda: same(vbuf, x, zm, right, 0, MAIN),
+            11: lambda: same(vbuf, x, zp, left, MAIN, REST),
             12: lambda: same(vbuf, x, zm, across),
             13: lambda: same(vbuf, x, zp, across),
-            14: lambda: same(vbuf, x, z2, across, 0, HALF),
-            15: lambda: same(vbuf, xn, zm, right, HALF, QUARTER),
-            31: lambda: same(vbuf, xn, zp, left, HALF + QUARTER, QUARTER),
+            14: lambda: same(vbuf, x, z2, across, 0, MAIN),
+            15: lambda: same(vbuf, xn, zm, right, MAIN, SIDES[0]),
+            31: lambda: same(vbuf, xn, zp, left, MAIN + SIDES[0], SIDES[1]),
             16: lambda: (kv(pk, x, z2), rk.at[h, 0], right),
             17: lambda: (kv(pk, xn, z2), rk.at[h, 1], left),
             18: lambda: (kv(pk, xn, zp), rk.at[h, 2], right),
@@ -118,14 +116,18 @@
             20: lambda: (kv(pk, x, zp), rk.at[h, 4], right),
             21: lambda: (kv(pk, xn, zm), rk.at[h, 5], left),
             22: lambda: (kv(pk, xn, z), rkx.at[h], across),
-            23: lambda: (kv(pv, xn, z2, 0, HALF), rvx.at[h, 0, pl.ds(0, HALF), :], across),
-            32: lambda: (kv(pv, xn, z2, HALF, QUARTER), rvq.at[h, 0], right),
-            33: lambda: (kv(pv, xn, z2, HALF + QUARTER, QUARTER), rvq.at[h, 1], left),
+            23: lambda: (kv(pv, xn, z2, 0, MAIN), rvx.at[h, 0, pl.ds(0, MAIN), :], across),
+            32: lambda: (kv(pv, xn, z2, MAIN, SIDES[0]), rvq.at[h, pl.ds(0, SIDES[0]), :], right),
+            33: lambda: (
+                kv(pv, xn, z2, MAIN + SIDES[0], SIDES[1]),
+                rvq.at[h, pl.ds(SIDES[0], SIDES[1]), :],
+                left,
+            ),
             24: lambda: (kv(pv, xn, zp), rvx.at[h, 1], across),
             25: lambda: (kv(pv, xn, zm), rvx.at[h, 2], across),
             26: lambda: (kv(pv, xn, z), rvx.at[h, 3], across),
-            27: lambda: (kv(pv, x, z2, 0, HALF), rvh.at[h, 0], right),
-            28: lambda: (kv(pv, x, z2, HALF, HALF), rvh.at[h, 1], left),
+            27: lambda: (kv(pv, x, z2, 0, MAIN), rvh.at[h, pl.ds(0, MAIN), :], right),
+            28: lambda: (kv(pv, x, z2, MAIN, REST), rvh.at[h, pl.ds(MAIN, REST), :], left),
             29: lambda: (kv(pv, x, zp), rvf.at[h, 0], right),
             30: lambda: (kv(pv, x, zm), rvf.at[h, 1], left),
         }[slot]()
@@ -153,11 +155,6 @@
             (vr_in.at[:, thin], vbuf.at[h, own, :]),
             (q_in.at[:, wide], q_vm.at[:, wide]),
             (do_in.at[:, wide], do_vm.at[:, wide]),
-            (dq_vm.at[:, wide], dq_out.at[:, wide]),
-            (small_vm.at[0, h], dkb_out.at[:, thin]),
-            (small_vm.at[1, h], dvb_out.at[:, thin]),
-            (root_vm.at[0, h], dkr_out.at[:, thin]),
-            (root_vm.at[1, h], dvr_out.at[:, thin]),
         )[which]
         return pltpu.make_async_copy(src, dst, lsem.at[h, which])
 
@@ -170,19 +167,24 @@
             total_here = total_here + f32(term)
         buf[h, here, :] = total_here.astype(BF16)
 
+    def sent(h, *slots):
+        for slot in slots:
+            copy(h, slot).wait_send()
+
     def pass_on(h, waits, sends):
         arrive(h, *waits)
         send(h, *sends)
 
     def value_side(h, side):
         arrive(h, 32 + side)
-        zi, first = ((zp, HALF), (zm, HALF + QUARTER))[side]
-        plus(pv, h, rows(xn, zi, first, QUARTER), rvq[h, side])
+        zi, first = ((zp, 0), (zm, SIDES[0]))[side]
+        came = rvq[h, first : first + SIDES[side]]
+        plus(pv, h, rows(xn, zi, MAIN + first, SIDES[side]), came)
         send(h, 24 + side)
 
     def value_half(h):
         arrive(h, 23)
-        plus(pv, h, rows(x, z2, 0, HALF), rvx[h, 0, :HALF])
+        plus(pv, h, rows(x, z2, 0, MAIN), rvx[h, 0, :MAIN])
         send(h, 27)
 
     def key_side(h, side):
@@ -193,9 +195,12 @@
     def value_block(h, side):
         arrive(h, 24 + side, 27 + side)
         zi = (zp, zm)[side]
-        first, other = ((0, HALF), (HALF, 0))[side]
-        plus(pv, h, rows(x, zi, first, HALF), rvx[h, 1 + side, first : first + HALF], rvh[h, side])
-        plus(pv, h, rows(x, zi, other, HALF), rvx[h, 1 + side, other : other + HALF])
+        both, alone = ((0, MAIN), (MAIN, REST))[:: 1 - 2 * side]
+        for (first, count), twice in ((both, True), (alone, False)):
+            came = [rvx[h, 1 + side, first : first + count]]
+            if twice:
+                came.append(rvh[h, first : first + count])
+            plus(pv, h, rows(x, zi, first, count), *came)
         send(h, 29 + side)
 
     def key_across(h):
@@ -205,17 +210,15 @@
 
     def value_out(h):
         arrive(h, 26, 29, 30)
-        root_vm[1, h] = (
+        dvr_out[:, head_cols(h)] = (
             f32(pv[h, rows(x, z), :]) + f32(rvx[h, 3]) + f32(rvf[h, 0]) + f32(rvf[h, 1])
         ).astype(BF16)
-        local(h, 8).start()
 
     def key_out(h):
         arrive(h, 19, 20, 22)
-        root_vm[0, h] = (
+        dkr_out[:, head_cols(h)] = (
             f32(pk[h, rows(x, z), :]) + f32(rk[h, 3]) + f32(rk[h, 4]) + f32(rkx[h])
         ).astype(BF16)
-        local(h, 7).start()
 
     steps = [
         lambda h: send(h, 0),
@@ -240,7 +243,13 @@
         key_across,
         value_out,
         key_out,
+        lambda h: late(),
     ]
+
+    def late():
+        back = (*range(16, 31), 32, 33)
+        for h in range(KVH):
+            sent(h, *(slot for slot in back if h < KVH - 1 or slot not in (22, 29, 30)))
 
     def run(piece, head):
         for number, h in PLAN.get((piece, head), ()):
@@ -421,14 +430,12 @@
 
             lax.fori_loop(0, 2, second_group, 0)
             dk, dv = second(h, even, kb_in[:, head_cols(h)], exp_own.at[even], dp_own.at[even], 0)
-            small_vm[0, h] = dk
-            small_vm[1, h] = dv
-            local(h, 5).start()
-            local(h, 6).start()
+            dkb_out[:, head_cols(h)] = dk
+            dvb_out[:, head_cols(h)] = dv
             for g in range(GROUP):
                 cols = pl.ds(pl.multiple_of((h * GROUP + g) * HD, HD), HD)
-                dq_vm[:, cols] = (dq_acc[:, g * TOK : (g + 1) * TOK].T * SCALE).astype(BF16)
-            local(h, 4).start()
+                dq_out[:, cols] = (dq_acc[:, g * TOK : (g + 1) * TOK].T * SCALE).astype(BF16)
+            sent(h, *range(16), 31)
             run_when(DONE, h)
 
         when(s > 0, second_half)
@@ -436,14 +443,7 @@
 
     lax.fori_loop(0, KVH + 1, step, 0)
 
-    def drain(h, carry):
-        for slot in range(SLOTS):
-            copy(h, slot).wait_send()
-        for which in range(4, 9):
-            local(h, which).wait()
-        return carry
-
-    lax.fori_loop(0, KVH, drain, 0)
+    sent(KVH - 1, 22, 29, 30)
 
 
 def hand_over(dq, dkb, dvb, dkr, dvr, dq_out, dkb_out, dvb_out, dkr_out, dvr_out, gone):
@@ -470,13 +470,10 @@
             buf((SHARD, KVH * HD), BF16),
         ),
         in_specs=[anywhere, vmem, vmem, anywhere, anywhere, anywhere, smem, smem],
-        out_specs=(anywhere,) * 5,
+        out_specs=(vmem,) * 5,
         scratch_shapes=[
             buf((TOK, KVH * NQ), BF16),
             buf((TOK, KVH * NQ), BF16),
-            buf((TOK, KVH * NQ), BF16),
-            buf((2, KVH, TOK, HD), BF16),
-            buf((2, KVH, SHARD, HD), BF16),
             buf((KVH, NQ, HD), BF16),
             buf((KVH, NQ, HD), BF16),
             buf((KVH, ROOT, HD), BF16),
@@ -486,9 +483,9 @@
             buf((KVH, 6, SHARD, HD), BF16),
             buf((KVH, SHARD, HD), BF16),
             buf((KVH, 4, SHARD, HD), BF16),
-            buf((KVH, 2, HALF, HD), BF16),
+            buf((KVH, SHARD, HD), BF16),
             buf((KVH, 2, SHARD, HD), BF16),
-            buf((KVH, 2, QUARTER, HD), BF16),
+            buf((KVH, REST, HD), BF16),
             buf((2, TOK, NQ), F32),
             buf((2, TOK, NQ), F32),
             buf((2, N_MEM, SHARD, NQ), F32),
@@ -501,7 +498,7 @@
             buf((1, NQ), jnp.int32),
             pltpu.SemaphoreType.DMA((KVH, SLOTS)),
             pltpu.SemaphoreType.DMA((KVH, SLOTS)),
-            pltpu.SemaphoreType.DMA((KVH, 9)),
+            pltpu.SemaphoreType.DMA((KVH, 4)),
         ],
         compiler_params=pltpu.CompilerParams(
             collective_id=0, has_side_effects=True, vmem_limit_bytes=60 * 2**20

time: 67.9 us -> 66.2 us (0.975)
  Pallas kernels: 67.1 us -> 65.4 us
    pallas_call x1, Pallas kernels: 65.9 us -> 64.2 us  [per_device(): pl.pallas_call(kernel, out_shape=(buf((TOK, KVH * GROUP * HD), BF16), buf...]
where the time goes in v3:
time: 66.2 us; the launch traced here: 66.1 us
  Pallas kernels  65.4 us (99%)
    pallas_call x1, Pallas kernels, per_device(): pl.pallas_call(kernel, out_shape=(buf((TOK, KVH * GROUP * HD), BF16), buf...  64.2 us

profile of v3, /device:TPU:0, one launch (start us, length us, event | category | flops | bytes accessed | tf_op | source)
XLA Modules:
  0.0 66.1 jit_solution(12351210375451571320)
XLA Ops:
  0.6 64.2 %shard_map.119 = (bf16[128,4096]{1,0:T(8,128)(2,1)S(1)}, bf16[128,512]{1,0:T(8,128)(2,1)S(1)}, bf16[128,512]{1,0:T(8,128)(2,1)S(1)}, bf16[256,512]{1,0:T(8,128)(2,1)S(1)}, bf16[256,512]{1,0:T(8,128)(2,1)S(1)}) custom-call(bf16[128,4096]{1,0:T(8,128)(2,1)} %q_in.1, bf16[128,512]{1,0:T(8,128)(2,1)} %kb_in.1, bf16[128,512]{1,0:T(8,128)(2,1)} %vb_in.1, ...), custom_call_target="tpu_custom_call" | custom-call | flops 12000000000 | bytes 6000000 | tf_op jit(solution)/shard_map/pallas_call | solution.py:463
  64.8 1.3 %shard_map.120 = (bf16[128,4096]{1,0:T(8,128)(2,1)}, bf16[128,512]{1,0:T(8,128)(2,1)}, bf16[128,512]{1,0:T(8,128)(2,1)}, bf16[256,512]{1,0:T(8,128)(2,1)}, bf16[256,512]{1,0:T(8,128)(2,1)}) custom-call(bf16[128,4096]{1,0:T(8,128)(2,1)S(1)} %get-tuple-element.10.dq, bf16[128,512]{1,0:T(8,128)(2,1)S(1)} %get-tuple-element.11.dkb, ...), custom_call_target="tpu_custom_call" | custom-call | tf_op jit(solution)/shard_map/pallas_call | solution.py:510

commit v4 on v3

--- a/solution.py
+++ b/solution.py
@@ -26,6 +26,7 @@
 SCALE = 1.0 / math.sqrt(HD)
 C2 = SCALE / math.log(2.0)
 SLOTS = 34
+FORWARD = 4
 START, OWN, NEAR_A, NEAR_B, FAR_A, FAR_B, BACK_A, BACK_B, BACK_C, BACK_D, DONE = range(11)
 PLAN = {
     (START, 0): [(1, 0), (0, 0), (3, 0), (1, 1), (2, 0), (0, 1), (5, 0), (4, 0), (6, 0)],
@@ -58,12 +59,12 @@
 
 
 def kernel(
-    q_in, kb_in, vb_in, kr_in, vr_in, do_in, len_in, fork_in,
+    q_in, kb_hbm, vb_hbm, kr_in, vr_in, do_in, len_hbm, fork_hbm,
     dq_out, dkb_out, dvb_out, dkr_out, dvr_out,
-    q_vm, do_vm,
+    q_vm, do_vm, kb_in, vb_in, len_in, fork_in,
     qs, gs, kbuf, vbuf, pk, pv, rk, rkx, rvx, rvh, rvf, rvq,
     exp_own, dp_own, exp_all, dp_all, maxes, total, corr, dq_acc, fork_row, start_row,
-    ssem, rsem, lsem,
+    ssem, rsem, lsem, isem,
 ):
     me = lax.axis_index("mem")
     x, z = me // RING, me % RING
@@ -268,9 +269,24 @@
         pl.semaphore_signal(
             barrier, inc=1, device_id={"mem": peer}, device_id_type=pl.DeviceIdType.MESH
         )
+    pl.semaphore_wait(barrier, 3)
+    for number, h in PLAN[START, 0]:
+        if number < FORWARD:
+            steps[number](h)
+    small = [
+        pltpu.make_async_copy(src, dst, isem.at[i])
+        for i, (src, dst) in enumerate(
+            ((len_hbm, len_in), (fork_hbm, fork_in), (kb_hbm, kb_in), (vb_hbm, vb_in))
+        )
+    ]
+    for one in small:
+        one.start()
     for h in range(KVH):
         for which in range(4):
             local(h, which).start()
+    for one in small:
+        one.wait()
+
     lens = [len_in[0, b] for b in range(4)]
     ends = [lens[0], lens[0] + lens[1], lens[0] + lens[1] + lens[2]]
     place = lax.broadcasted_iota(jnp.int32, (1, NQ), 1) % TOK
@@ -294,8 +310,9 @@
     for h in range(KVH):
         local(h, 0).wait()
         local(h, 1).wait()
-    pl.semaphore_wait(barrier, 3)
-    run(START, 0)
+    for number, h in PLAN[START, 0]:
+        if number >= FORWARD:
+            steps[number](h)
 
     order = [
         (x, z), (xn, z), (x, zp), (x, zm), (xn, zp), (xn, zm), (x, z2), (xn, z2),
@@ -456,9 +473,7 @@
 
 
 def per_device(*args):
-    vmem, anywhere, smem = (
-        pl.BlockSpec(memory_space=space) for space in (pltpu.VMEM, pl.ANY, pltpu.SMEM)
-    )
+    vmem, anywhere = (pl.BlockSpec(memory_space=space) for space in (pltpu.VMEM, pl.ANY))
     buf = pltpu.VMEM
     outs = pl.pallas_call(
         kernel,
@@ -469,11 +484,15 @@
             buf((SHARD, KVH * HD), BF16),
             buf((SHARD, KVH * HD), BF16),
         ),
-        in_specs=[anywhere, vmem, vmem, anywhere, anywhere, anywhere, smem, smem],
+        in_specs=[anywhere] * 8,
         out_specs=(vmem,) * 5,
         scratch_shapes=[
             buf((TOK, KVH * NQ), BF16),
             buf((TOK, KVH * NQ), BF16),
+            buf((TOK, KVH * HD), BF16),
+            buf((TOK, KVH * HD), BF16),
+            pltpu.SMEM((1, 4), jnp.int32),
+            pltpu.SMEM((1, 4), jnp.int32),
             buf((KVH, NQ, HD), BF16),
             buf((KVH, NQ, HD), BF16),
             buf((KVH, ROOT, HD), BF16),
@@ -499,6 +518,7 @@
             pltpu.SemaphoreType.DMA((KVH, SLOTS)),
             pltpu.SemaphoreType.DMA((KVH, SLOTS)),
             pltpu.SemaphoreType.DMA((KVH, 4)),
+            pltpu.SemaphoreType.DMA((4,)),
         ],
         compiler_params=pltpu.CompilerParams(
             collective_id=0, has_side_effects=True, vmem_limit_bytes=60 * 2**20

time: 66.2 us -> 65.1 us (0.983)
  Pallas kernels: 65.4 us -> 64.3 us
    pallas_call x1, Pallas kernels: 64.2 us -> 63.1 us  [per_device(): pl.pallas_call(kernel, out_shape=(buf((TOK, KVH * GROUP * HD), BF16), buf...]
where the time goes in v4:
time: 65.1 us; the launch traced here: 65 us
  Pallas kernels  64.3 us (99%)
    pallas_call x1, Pallas kernels, per_device(): pl.pallas_call(kernel, out_shape=(buf((TOK, KVH * GROUP * HD), BF16), buf...  63.1 us

profile of v4, /device:TPU:0, one launch (start us, length us, event | category | flops | bytes accessed | tf_op | source)
XLA Modules:
  0.0 65.0 jit_solution(1020057862729983444)
XLA Ops:
  0.6 63.1 %shard_map.119 = (bf16[128,4096]{1,0:T(8,128)(2,1)S(1)}, bf16[128,512]{1,0:T(8,128)(2,1)S(1)}, bf16[128,512]{1,0:T(8,128)(2,1)S(1)}, bf16[256,512]{1,0:T(8,128)(2,1)S(1)}, bf16[256,512]{1,0:T(8,128)(2,1)S(1)}) custom-call(bf16[128,4096]{1,0:T(8,128)(2,1)} %q_in.1, bf16[128,512]{1,0:T(8,128)(2,1)} %kb_hbm.1, bf16[128,512]{1,0:T(8,128)(2,1)} %vb_hbm.1, ...), custom_call_target="tpu_custom_call" | custom-call | flops 12000000000 | bytes 6000000 | tf_op jit(solution)/shard_map/pallas_call | solution.py:478
  63.7 1.3 %shard_map.120 = (bf16[128,4096]{1,0:T(8,128)(2,1)}, bf16[128,512]{1,0:T(8,128)(2,1)}, bf16[128,512]{1,0:T(8,128)(2,1)}, bf16[256,512]{1,0:T(8,128)(2,1)}, bf16[256,512]{1,0:T(8,128)(2,1)}) custom-call(bf16[128,4096]{1,0:T(8,128)(2,1)S(1)} %get-tuple-element.10.dq, bf16[128,512]{1,0:T(8,128)(2,1)S(1)} %get-tuple-element.11.dkb, ...), custom_call_target="tpu_custom_call" | custom-call | tf_op jit(solution)/shard_map/pallas_call | solution.py:530

commit v5 on v4

--- a/solution.py
+++ b/solution.py
@@ -465,7 +465,13 @@
 
 def hand_over(dq, dkb, dvb, dkr, dvr, dq_out, dkb_out, dvb_out, dkr_out, dvr_out, gone):
     srcs, dsts = (dq, dkb, dvb, dkr, dvr), (dq_out, dkb_out, dvb_out, dkr_out, dvr_out)
-    outs = [pltpu.make_async_copy(a, b, gone.at[i]) for i, (a, b) in enumerate(zip(srcs, dsts))]
+    outs = []
+    for src, dst in zip(srcs, dsts):
+        parts = max(1, src.size // (SHARD * KVH * HD))
+        count = src.shape[0] // parts
+        for part in range(parts):
+            here = pl.ds(part * count, count)
+            outs.append(pltpu.make_async_copy(src.at[here], dst.at[here], gone.at[len(outs)]))
     for one in outs:
         one.start()
     for one in outs:
@@ -532,7 +538,7 @@
         out_shape=tuple(jax.ShapeDtypeStruct(out.shape, out.dtype) for out in outs),
         in_specs=[anywhere] * 5,
         out_specs=(anywhere,) * 5,
-        scratch_shapes=[pltpu.SemaphoreType.DMA((5,))],
+        scratch_shapes=[pltpu.SemaphoreType.DMA((8,))],
     )(*[pltpu.with_memory_space_constraint(out, pltpu.VMEM) for out in outs])
 
 

time: 65.1 us -> 65.2 us (level)
  no operation moved by 1% of the time
where the time goes in v5:
time: 65.2 us; the launch traced here: 65 us
  Pallas kernels  64.4 us (99%)
    pallas_call x1, Pallas kernels, per_device(): pl.pallas_call(kernel, out_shape=(buf((TOK, KVH * GROUP * HD), BF16), buf...  63.1 us

profile of v5, /device:TPU:0, one launch (start us, length us, event | category | flops | bytes accessed | tf_op | source)
XLA Modules:
  0.0 65.0 jit_solution(830741494356672252)
XLA Ops:
  0.6 63.1 %shard_map.119 = (bf16[128,4096]{1,0:T(8,128)(2,1)S(1)}, bf16[128,512]{1,0:T(8,128)(2,1)S(1)}, bf16[128,512]{1,0:T(8,128)(2,1)S(1)}, bf16[256,512]{1,0:T(8,128)(2,1)S(1)}, bf16[256,512]{1,0:T(8,128)(2,1)S(1)}) custom-call(bf16[128,4096]{1,0:T(8,128)(2,1)} %q_in.1, bf16[128,512]{1,0:T(8,128)(2,1)} %kb_hbm.1, bf16[128,512]{1,0:T(8,128)(2,1)} %vb_hbm.1, ...), custom_call_target="tpu_custom_call" | custom-call | flops 12000000000 | bytes 6000000 | tf_op jit(solution)/shard_map/pallas_call | solution.py:484
  63.7 1.3 %shard_map.120 = (bf16[128,4096]{1,0:T(8,128)(2,1)}, bf16[128,512]{1,0:T(8,128)(2,1)}, bf16[128,512]{1,0:T(8,128)(2,1)}, bf16[256,512]{1,0:T(8,128)(2,1)}, bf16[256,512]{1,0:T(8,128)(2,1)}) custom-call(bf16[128,4096]{1,0:T(8,128)(2,1)S(1)} %get-tuple-element.10.dq, bf16[128,512]{1,0:T(8,128)(2,1)S(1)} %get-tuple-element.11.dkb, ...), custom_call_target="tpu_custom_call" | custom-call | tf_op jit(solution)/shard_map/pallas_call | solution.py:536
